TPU v7x, 32 devices: a whole 2x2x4 slice. The times are simulated.
32 devices in a mesh: groups: 2 (over y), rows: 4 (over z), tm: 2 (over x), cols: 2 (over core).
Axes of the slice: x: 2, y: 2, z: 4, core: 2. Of those that a mesh axis runs over, the one named last changes fastest.
Arguments:
- latents: bfloat16 [20, 4, 80, 384], P(('groups', 'tm'), 'rows', 'cols'), parts along dimension 0, may hold values from -16 to 16
- gain_one: float32 [384], replicated, may hold values from 0.1 to 1.9
- conv_one: bfloat16 [27, 384, 384], P(None, 'rows'), may hold values from -0.0625 to 0.0625
- bias_one: float32 [384], replicated, may hold values from -3 to 3
- gain_two: float32 [384], replicated, may hold values from 0.1 to 1.9
- conv_two: bfloat16 [27, 384, 384], P(None, 'rows'), may hold values from -0.0625 to 0.0625
- bias_two: float32 [384], replicated, may hold values from -3 to 3
Outputs:
- block_out: bfloat16 [20, 4, 80, 384], P(('groups', 'tm'), 'rows', 'cols'), parts along dimension 0
There are 2 independent parts, one for each index of `groups`. A program takes and returns all parts, laid end to end along the dimension named above; an argument that names none is the same for every part. Nothing has to cross between parts.
All inputs are finite; a program needn't handle non-finite values.
Results may differ from a plain program's by a relative error of at most 0.006.
Values may be sent and summed in bfloat16 or wider, within the bound.
A program may use at most 64 MiB of HBM per device.

v0:
```python
import jax
import jax.numpy as jnp
from jax import lax
from jax.sharding import PartitionSpec as P


def with_halo(cells, sides, width):
    for axis, dim in sides:
        count = lax.axis_size(axis)
        ends = count - 1
        head = lax.slice_in_dim(cells, 0, width, axis=dim)
        tail = lax.slice_in_dim(cells, cells.shape[dim] - width, cells.shape[dim], axis=dim)
        cells = jnp.concatenate(
            [
                lax.ppermute(tail, axis, [(i, (i + 1) % count) for i in range(ends)]),
                cells,
                lax.ppermute(head, axis, [((i + 1) % count, i) for i in range(ends)]),
            ],
            axis=dim,
        )
    return cells


def passed_along(block, axis, distance):
    devices = range(lax.axis_size(axis))
    route = [(i - distance, i) for i in devices if i - distance in devices]
    return lax.ppermute(block, axis, route)


def activate(values, gain_values):
    values = values.astype(jnp.float32)
    mean_square = jnp.mean(values * values, axis=-1, keepdims=True)
    return jax.nn.silu(values * lax.rsqrt(mean_square + 1e-06) * gain_values).astype(jnp.bfloat16)


def tap_sum(padded, weight_part, frames, height, breadth):
    channels = padded.shape[3]
    summed = jnp.zeros((frames * height * breadth, weight_part.shape[1]), jnp.float32)
    for depth_tap in range(3):
        for row_tap in range(3):
            for col_tap in range(3):
                window = padded[
                    depth_tap : depth_tap + frames,
                    row_tap : row_tap + height,
                    col_tap : col_tap + breadth,
                ]
                window = window.reshape(frames * height * breadth, channels)
                kernel = weight_part[9 * depth_tap + 3 * row_tap + col_tap]
                summed = summed + lax.dot_general(
                    window, kernel, (((1,), (1,)), ((), ())), preferred_element_type=jnp.float32
                )
    return summed


def convolve(extended, weight, bias_values):
    frames = extended.shape[0] - 2
    breadth = extended.shape[2]
    with_sides = with_halo(extended, (("cols", 2),), 1)
    column = lax.all_gather(with_sides, "rows", axis=1, tiled=True)
    padded = jnp.pad(column, ((0, 0), (1, 1), (0, 0), (0, 0)))
    full_height = column.shape[1]
    slice_width = weight.shape[1]
    offset = lax.axis_index("rows") * slice_width
    summed = tap_sum(padded, weight, frames, full_height, breadth)
    summed = summed + lax.dynamic_slice_in_dim(bias_values, offset, slice_width)
    result = summed.reshape(frames, full_height, breadth, slice_width)
    return lax.all_to_all(result, "rows", split_axis=1, concat_axis=3, tiled=True)


def with_past(inputs):
    earlier = passed_along(inputs[-2:], "tm", 1)
    return jnp.concatenate([earlier, inputs], axis=0)


def shards(latents, gain_one, conv_one, bias_one, gain_two, conv_two, bias_two):
    first_act = activate(latents, gain_one)
    first_out = convolve(with_past(first_act), conv_one, bias_one).astype(jnp.bfloat16)
    second_act = activate(first_out, gain_two)
    branch = convolve(with_past(second_act), conv_two, bias_two)
    return (latents.astype(jnp.float32) + branch).astype(jnp.bfloat16)


def solution(mesh):
    return jax.shard_map(
        shards,
        mesh=mesh,
        in_specs=(
            P(("groups", "tm"), "rows", "cols", None),
            P(),
            P(None, "rows", None),
            P(),
            P(),
            P(None, "rows", None),
            P(),
        ),
        out_specs=P(("groups", "tm"), "rows", "cols", None),
        check_vma=False,
    )
```

profile of v0, /device:TPU:0, one launch (start us, length us, event | category | flops | bytes accessed | tf_op | source)
XLA Modules:
  0.0 121.3 jit_solution(12247536379900046480)
XLA Ops:
  0.0 1.0 fusion.3
  1.0 1.1 fusion.10
  2.1 4.8 %collective-permute-start = (bf16[2,1,40,384]{3,2,1,0:T(8,128)(2,1)S(1)}, bf16[2,1,40,384]{3,2,1,0:T(8,128)(2,1)S(1)}, u32[]{:S(2)}, u32[]{:S(2)}) collective-permute-start(bf16[2,1,40,384]{3,2,1,0:T(8,128)(2,1)S(1)} %slice.474), channel_id=1, source_target_pairs={{0,2},{1,3},{4,6},{5,7},{8,10},{9,11},{12,14},{13,15},{16,18},{17,... | collective-permute-start | bytes 184328 | tf_op jit(solution)/shard_map/ppermute | solution.py:27
  7.0 1.8 %collective-permute-done = bf16[2,1,40,384]{3,2,1,0:T(8,128)(2,1)S(1)} collective-permute-done((bf16[2,1,40,384]{3,2,1,0:T(8,128)(2,1)S(1)}, bf16[2,1,40,384]{3,2,1,0:T(8,128)(2,1)S(1)}, u32[]{:S(2)}, u32[]{:S(2)}) %collective-permute-start) | collective-permute-done | bytes 61472 | tf_op jit(solution)/shard_map/ppermute | solution.py:27
  8.9 1.3 %collective-permute-start.2 = (bf16[7,1,1,384]{3,2,1,0:T(2,128)(2,1)S(1)}, bf16[7,1,1,384]{3,2,1,0:T(2,128)(2,1)S(1)}, u32[]{:S(2)}, u32[]{:S(2)}) collective-permute-start(bf16[7,1,1,384]{3,2,1,0:T(2,128)(2,1)S(1)} %get-tuple-element.62), channel_id=1, source_target_pairs={{1,0},{3,2},{5,4},{7,6},{9,8},{11,10},{13,12},{15,14},{17,16},{19,... | collective-permute-start | bytes 16136 | tf_op jit(solution)/shard_map/ppermute | solution.py:17
  10.2 3.0 %collective-permute-start.1 = (bf16[7,1,1,384]{3,2,1,0:T(2,128)(2,1)S(1)}, bf16[7,1,1,384]{3,2,1,0:T(2,128)(2,1)S(1)}, u32[]{:S(2)}, u32[]{:S(2)}) collective-permute-start(bf16[7,1,1,384]{3,2,1,0:T(2,128)(2,1)S(1)} %get-tuple-element.61), channel_id=1, source_target_pairs={{0,1},{2,3},{4,5},{6,7},{8,9},{10,11},{12,13},{14,15},{16,17},{18,... | collective-permute-start | bytes 16136 | tf_op jit(solution)/shard_map/ppermute | solution.py:15
  13.2 0.8 dynamic_slice.6
  14.1 22.6 %all_gather.6 = bf16[7,4,42,384]{3,2,1,0:T(8,128)(2,1)S(1)} all-gather(bf16[7,1,42,384]{3,2,1,0:T(8,128)(2,1)S(1)} %pad_maximum_fusion), channel_id=1, replica_groups=mesh['groups'=2,'rows'=4,'tm'=2,'cols'=2] {'rows'}, dimensions={1}, use_global_device_ids=true | all-gather | bytes 1128960 | tf_op jit(solution)/shard_map/all_gather | solution.py:59
  36.7 0.6 fusion.124
  37.3 2.3 %pad_slice_fusion.18 = (bf16[5,4,40,384]{3,2,1,0:T(8,128)(2,1)S(1)}, bf16[5,4,40,384]{3,2,1,0:T(8,128)(2,1)S(1)}, bf16[5,4,40,384]{3,2,1,0:T(8,128)(2,1)S(1)}, b...) fusion(bf16[7,4,42,384]{3,2,1,0:T(8,128)(2,1)S(1)} %all_gather.6), kind=kLoop, calls=%fused_computation.18 | loop fusion | bytes 13934592 | tf_op jit(solution)/shard_map/slice | solution.py:42
  44.6 0.3 convolution_add_fusion.37
  48.2 0.3 fusion
  48.8 11.3 %all_to_all.27 = bf16[5,4,40,96]{3,2,0,1:T(8,128)(2,1)S(1)} all-to-all(bf16[5,4,40,96]{3,2,0,1:T(8,128)(2,1)S(1)} %copy.25), channel_id=1, replica_groups=mesh['groups'=2,'rows'=4,'tm'=2,'cols'=2] {'rows'}, dimensions={1} | all-to-all | bytes 307200 | tf_op jit(solution)/shard_map/all_to_all | solution.py:67
  60.8 4.3 %collective-permute-start.3 = (bf16[2,1,40,384]{3,2,1,0:T(8,128)(2,1)S(1)}, bf16[2,1,40,384]{3,2,1,0:T(8,128)(2,1)S(1)}, u32[]{:S(2)}, u32[]{:S(2)}) collective-permute-start(bf16[2,1,40,384]{3,2,1,0:T(8,128)(2,1)S(1)} %slice.484), channel_id=1, source_target_pairs={{0,2},{1,3},{4,6},{5,7},{8,10},{9,11},{12,14},{13,15},{16,18},{17,... | collective-permute-start | bytes 184328 | tf_op jit(solution)/shard_map/ppermute | solution.py:27
  65.0 1.8 %collective-permute-done.3 = bf16[2,1,40,384]{3,2,1,0:T(8,128)(2,1)S(1)} collective-permute-done((bf16[2,1,40,384]{3,2,1,0:T(8,128)(2,1)S(1)}, bf16[2,1,40,384]{3,2,1,0:T(8,128)(2,1)S(1)}, u32[]{:S(2)}, u32[]{:S(2)}) %collective-permute-start.3) | collective-permute-done | bytes 61472 | tf_op jit(solution)/shard_map/ppermute | solution.py:27
  66.9 1.3 %collective-permute-start.5 = (bf16[7,1,1,384]{3,2,1,0:T(2,128)(2,1)S(1)}, bf16[7,1,1,384]{3,2,1,0:T(2,128)(2,1)S(1)}, u32[]{:S(2)}, u32[]{:S(2)}) collective-permute-start(bf16[7,1,1,384]{3,2,1,0:T(2,128)(2,1)S(1)} %get-tuple-element.60), channel_id=1, source_target_pairs={{1,0},{3,2},{5,4},{7,6},{9,8},{11,10},{13,12},{15,14},{17,16},{19,... | collective-permute-start | bytes 16136 | tf_op jit(solution)/shard_map/ppermute | solution.py:17
  68.2 3.0 %collective-permute-start.4 = (bf16[7,1,1,384]{3,2,1,0:T(2,128)(2,1)S(1)}, bf16[7,1,1,384]{3,2,1,0:T(2,128)(2,1)S(1)}, u32[]{:S(2)}, u32[]{:S(2)}) collective-permute-start(bf16[7,1,1,384]{3,2,1,0:T(2,128)(2,1)S(1)} %get-tuple-element.59), channel_id=1, source_target_pairs={{0,1},{2,3},{4,5},{6,7},{8,9},{10,11},{12,13},{14,15},{16,17},{18,... | collective-permute-start | bytes 16136 | tf_op jit(solution)/shard_map/ppermute | solution.py:15
  71.2 0.8 dynamic_slice.7
  72.1 21.8 %all_gather.7 = bf16[7,4,42,384]{3,2,1,0:T(8,128)(2,1)S(1)} all-gather(bf16[7,1,42,384]{3,2,1,0:T(8,128)(2,1)S(1)} %pad_maximum_fusion.1), channel_id=1, replica_groups=mesh['groups'=2,'rows'=4,'tm'=2,'cols'=2] {'rows'}, dimensions={1}, use_global_device_ids=true | all-gather | bytes 1128960 | tf_op jit(solution)/shard_map/all_gather | solution.py:59
  93.9 0.6 fusion.123
  94.5 2.3 %pad_slice_fusion = (bf16[5,4,40,384]{3,2,1,0:T(8,128)(2,1)S(1)}, bf16[5,4,40,384]{3,2,1,0:T(8,128)(2,1)S(1)}, bf16[5,4,40,384]{3,2,1,0:T(8,128)(2,1)S(1)}, bf16...) fusion(bf16[7,4,42,384]{3,2,1,0:T(8,128)(2,1)S(1)} %all_gather.7), kind=kLoop, calls=%fused_computation | loop fusion | bytes 13934592 | tf_op jit(solution)/shard_map/slice | solution.py:42
  105.5 0.3 fusion.1
  106.0 14.2 %all_to_all.28 = f32[5,4,40,96]{3,2,0,1:T(8,128)S(1)} all-to-all(f32[5,4,40,96]{3,2,0,1:T(8,128)S(1)} %copy.29), channel_id=1, replica_groups=mesh['groups'=2,'rows'=4,'tm'=2,'cols'=2] {'rows'}, dimensions={1} | all-to-all | bytes 614400 | tf_op jit(solution)/shard_map/all_to_all | solution.py:67
  120.6 0.7 fusion.11
  (82 shorter events, 18.3 us)
Async XLA Ops:
  2.1 6.7 %collective-permute-start = (bf16[2,1,40,384]{3,2,1,0:T(8,128)(2,1)S(1)}, bf16[2,1,40,384]{3,2,1,0:T(8,128)(2,1)S(1)}, u32[]{:S(2)}, u32[]{:S(2)}) collective-permute-start(bf16[2,1,40,384]{3,2,1,0:T(8,128)(2,1)S(1)} %slice.474), channel_id=1, source_target_pairs={{0,2},{1,3},{4,6},{5,7},{8,10},{9,11},{12,14},{13,15},{16,18},{17,... | collective-permute-start | bytes 184328 | tf_op jit(solution)/shard_map/ppermute | solution.py:27
  8.9 5.1 %collective-permute-start.2 = (bf16[7,1,1,384]{3,2,1,0:T(2,128)(2,1)S(1)}, bf16[7,1,1,384]{3,2,1,0:T(2,128)(2,1)S(1)}, u32[]{:S(2)}, u32[]{:S(2)}) collective-permute-start(bf16[7,1,1,384]{3,2,1,0:T(2,128)(2,1)S(1)} %get-tuple-element.62), channel_id=1, source_target_pairs={{1,0},{3,2},{5,4},{7,6},{9,8},{11,10},{13,12},{15,14},{17,16},{19,... | collective-permute-start | bytes 16136 | tf_op jit(solution)/shard_map/ppermute | solution.py:17
  10.2 3.8 %collective-permute-start.1 = (bf16[7,1,1,384]{3,2,1,0:T(2,128)(2,1)S(1)}, bf16[7,1,1,384]{3,2,1,0:T(2,128)(2,1)S(1)}, u32[]{:S(2)}, u32[]{:S(2)}) collective-permute-start(bf16[7,1,1,384]{3,2,1,0:T(2,128)(2,1)S(1)} %get-tuple-element.61), channel_id=1, source_target_pairs={{0,1},{2,3},{4,5},{6,7},{8,9},{10,11},{12,13},{14,15},{16,17},{18,... | collective-permute-start | bytes 16136 | tf_op jit(solution)/shard_map/ppermute | solution.py:15
  37.3 2.3 %copy-start = (bf16[27,96,384]{2,1,0:T(8,128)(2,1)S(1)}, bf16[27,96,384]{2,1,0:T(8,128)(2,1)}, u32[]{:S(2)}) copy-start(bf16[27,96,384]{2,1,0:T(8,128)(2,1)} %param.9) | copy-start | bytes 5971972
  48.5 12.0 %copy-start.3 = (f32[384]{0:T(512)S(1)}, f32[384]{0:T(512)}, u32[]{:S(2)}) copy-start(f32[384]{0:T(512)} %param.11) | copy-start | bytes 4612
  60.8 6.1 %collective-permute-start.3 = (bf16[2,1,40,384]{3,2,1,0:T(8,128)(2,1)S(1)}, bf16[2,1,40,384]{3,2,1,0:T(8,128)(2,1)S(1)}, u32[]{:S(2)}, u32[]{:S(2)}) collective-permute-start(bf16[2,1,40,384]{3,2,1,0:T(8,128)(2,1)S(1)} %slice.484), channel_id=1, source_target_pairs={{0,2},{1,3},{4,6},{5,7},{8,10},{9,11},{12,14},{13,15},{16,18},{17,... | collective-permute-start | bytes 184328 | tf_op jit(solution)/shard_map/ppermute | solution.py:27
  66.9 5.1 %collective-permute-start.5 = (bf16[7,1,1,384]{3,2,1,0:T(2,128)(2,1)S(1)}, bf16[7,1,1,384]{3,2,1,0:T(2,128)(2,1)S(1)}, u32[]{:S(2)}, u32[]{:S(2)}) collective-permute-start(bf16[7,1,1,384]{3,2,1,0:T(2,128)(2,1)S(1)} %get-tuple-element.60), channel_id=1, source_target_pairs={{1,0},{3,2},{5,4},{7,6},{9,8},{11,10},{13,12},{15,14},{17,16},{19,... | collective-permute-start | bytes 16136 | tf_op jit(solution)/shard_map/ppermute | solution.py:17
  68.2 3.8 %collective-permute-start.4 = (bf16[7,1,1,384]{3,2,1,0:T(2,128)(2,1)S(1)}, bf16[7,1,1,384]{3,2,1,0:T(2,128)(2,1)S(1)}, u32[]{:S(2)}, u32[]{:S(2)}) collective-permute-start(bf16[7,1,1,384]{3,2,1,0:T(2,128)(2,1)S(1)} %get-tuple-element.59), channel_id=1, source_target_pairs={{0,1},{2,3},{4,5},{6,7},{8,9},{10,11},{12,13},{14,15},{16,17},{18,... | collective-permute-start | bytes 16136 | tf_op jit(solution)/shard_map/ppermute | solution.py:15
  94.5 2.3 %copy-start.1 = (bf16[27,96,384]{2,1,0:T(8,128)(2,1)S(1)}, bf16[27,96,384]{2,1,0:T(8,128)(2,1)}, u32[]{:S(2)}) copy-start(bf16[27,96,384]{2,1,0:T(8,128)(2,1)} %param.12) | copy-start | bytes 5971972
  105.8 14.8 %copy-start.2 = (bf16[5,1,40,384]{3,2,1,0:T(8,128)(2,1)S(1)}, bf16[5,1,40,384]{3,2,1,0:T(8,128)(2,1)}, u32[]{:S(2)}) copy-start(bf16[5,1,40,384]{3,2,1,0:T(8,128)(2,1)} %param.7) | copy-start | bytes 460804
where the time goes:
time: 122 us; the launch traced here: 121 us
  blocking collectives  69.9 us (57%)
  starting transfers between devices  17.7 us (15%)
  matrix products  17.6 us (14%)
  local copies, waits for them, and re-layouts  8.33 us (7%)
  waiting for transfers between devices  3.79 us (3%)
  other arithmetic  3.34 us (3%)
    all_gather x2, blocking collectives, convolve(): column = lax.all_gather(with_sides, 'rows', axis=1, tiled=True)  44.4 us
    all_to_all x2, blocking collectives, convolve(): lax.all_to_all(result, 'rows', split_axis=1, concat_axis=3, tiled=True)  25.5 us
    dot_general x54, matrix products, tap_sum(): lax.dot_general(window, kernel, (((1,), (1,)), ((), ())), preferred_eleme...  17.6 us
    ppermute x2, starting transfers between devices, passed_along(): return lax.ppermute(block, axis, route)  9.1 us
    ppermute x2, starting transfers between devices, with_halo(): lax.ppermute(tail, axis, [(i, (i + 1) % count) for i in range(ends)])  6.05 us
    slice x4, local copies, waits for them, and re-layouts, tap_sum(): padded[depth_tap:depth_tap + frames, row_tap:row_tap + height, col_tap:co...  5.72 us
    ppermute x2, waiting for transfers between devices, passed_along(): return lax.ppermute(block, axis, route)  3.69 us
    ppermute x2, starting transfers between devices, with_halo(): lax.ppermute(head, axis, [((i + 1) % count, i) for i in range(ends)])  2.58 us
  transfers between devices with their start and end apart: 6, of which 2 were waited for; matrix products, arithmetic and copies ran while one was open for 1% of the time, Pallas kernels for 0%

commit v1 on v0

v1 whole, which is shorter than its diff:
```python
import functools

import jax
import jax.numpy as jnp
from jax import lax
from jax.experimental import pallas as pl
from jax.experimental.pallas import tpu as pltpu
from jax.sharding import PartitionSpec as P

MESH = pl.DeviceIdType.MESH
EPS = 1e-06


def up(value, multiple):
    return -(-value // multiple) * multiple


def activate(values, gain_values):
    mean_square = jnp.mean(values * values, axis=-1, keepdims=True)
    return jax.nn.silu(values * lax.rsqrt(mean_square + EPS) * gain_values)


def kernel(
    n_rows, n_tm, n_out,
    x_ref, g1_ref, w1_ref, b1_ref, g2_ref, w2_ref, b2_ref, out_ref,
    abuf, wbuf, zbuf, obuf, osend, psend, orecv, precv, edge_out, edge_in,
    w_sem, a_send, a_recv, e_send, e_recv, o_send, o_recv, p_send, p_recv,
):
    frames, _, width, chans = x_ref.shape
    cells = frames * width
    block = abuf.shape[2]
    head = block - 16
    lanes = wbuf.shape[3]
    r = lax.axis_index("rows")
    t = lax.axis_index("tm")
    c = lax.axis_index("cols")
    weights = (w1_ref, w2_ref)
    gains = (g1_ref, g2_ref)
    biases = (b1_ref, b2_ref)
    has_next = t + 1 < n_tm
    has_prev = t > 0
    distances = sorted(range(1, n_rows), key=lambda d: min(d, n_rows - d))

    def weight_copy(v, row_tap):
        return pltpu.make_async_copy(
            weights[v].at[:, row_tap],
            wbuf.at[v, :, :, pl.ds(0, weights[v].shape[3]), pl.ds(row_tap * chans, chans)],
            w_sem.at[v, row_tap],
        )

    for v in range(2):
        for row_tap in range(3):
            weight_copy(v, row_tap).start()

    barrier = pltpu.get_barrier_semaphore()

    def greet(where):
        pl.semaphore_signal(barrier, inc=1, device_id=where, device_id_type=MESH)

    for d in distances:
        greet({"rows": lax.rem(r + d, n_rows)})
    greet({"cols": 1 - c})

    @pl.when(has_next)
    def _():
        for j in range(n_rows):
            greet({"rows": j, "tm": t + 1})

    @pl.when(has_prev)
    def _():
        for j in range(n_rows):
            greet({"rows": j, "tm": t - 1})

    filled = weights[0].shape[3]
    for v in range(2):
        abuf[v, 0] = jnp.zeros((block, chans), jnp.bfloat16)
        abuf[v, n_rows + 1] = jnp.zeros((block, chans), jnp.bfloat16)
        if filled < lanes:
            wbuf[v, :, :, filled:, :] = jnp.zeros((3, 3, lanes - filled, 3 * chans), jnp.bfloat16)

    @pl.when(t == 0)
    def _():
        precv[...] = jnp.zeros(precv.shape, precv.dtype)

    def edge_copy(v):
        return pltpu.make_async_remote_copy(
            src_ref=edge_out.at[v], dst_ref=edge_in.at[v],
            send_sem=e_send.at[v], recv_sem=e_recv.at[v],
            device_id={"cols": 1 - c}, device_id_type=MESH,
        )

    def span(piece):
        return pl.ds(0, head) if piece == 0 else pl.ds(head, 16)

    def act_send(v, piece, d):
        part = abuf.at[v, r + 1, span(piece)]
        return pltpu.make_async_remote_copy(
            src_ref=part, dst_ref=part,
            send_sem=a_send.at[v, piece, d], recv_sem=a_recv.at[v, piece, r],
            device_id={"rows": lax.rem(r + d, n_rows)}, device_id_type=MESH,
        )

    def act_arrival(v, piece, j):
        part = abuf.at[v, j + 1, span(piece)]
        return pltpu.make_async_remote_copy(
            src_ref=part, dst_ref=part,
            send_sem=a_send.at[v, piece, 0], recv_sem=a_recv.at[v, piece, j],
            device_id={"rows": j}, device_id_type=MESH,
        )

    def out_copy(v, h, source):
        return pltpu.make_async_remote_copy(
            src_ref=osend.at[v, h], dst_ref=orecv.at[v, source],
            send_sem=o_send.at[v, h], recv_sem=o_recv.at[v, source],
            device_id={"rows": h}, device_id_type=MESH,
        )

    def past_copy(v, h, source):
        return pltpu.make_async_remote_copy(
            src_ref=psend.at[v, h], dst_ref=precv.at[v, source],
            send_sem=p_send.at[v, h], recv_sem=p_recv.at[v, source],
            device_id={"rows": h, "tm": t + 1}, device_id_type=MESH,
        )

    def spread(v, act):
        cube = act.reshape(frames, width, chans)
        edge = jnp.where(c == 0, cube[:, width - 1, :], cube[:, 0, :])
        edge = jnp.concatenate([edge, jnp.zeros((16 - frames, chans), jnp.float32)], axis=0)
        edge_out[v] = edge.astype(jnp.bfloat16)
        if v == 0:
            pl.semaphore_wait(
                barrier,
                n_rows + jnp.where(has_next, n_rows, 0) + jnp.where(has_prev, n_rows, 0),
            )
        edge_copy(v).start()
        abuf[v, r + 1, 0:head] = act[0:head].astype(jnp.bfloat16)
        for d in distances:
            act_send(v, 0, d).start()
        edge_copy(v).wait_recv()
        got = edge_in[v].astype(jnp.float32)
        last = jnp.concatenate([act[head:cells], got[0 : block - cells]], axis=0)
        abuf[v, r + 1, head:block] = last.astype(jnp.bfloat16)
        for d in distances:
            act_send(v, 1, d).start()

    def convolve(v):
        bias = jnp.zeros((1, n_out), jnp.float32)
        for j in range(n_rows):
            bias = bias + jnp.where(r == j, biases[v][:, j * n_out : (j + 1) * n_out], 0.0)
        if n_out < lanes:
            bias = jnp.concatenate([bias, jnp.zeros((1, lanes - n_out), jnp.float32)], axis=1)
        column = lax.broadcasted_iota(jnp.int32, (width, lanes), 0)
        edge_column = jnp.where(c == 0, width - 1, 0)
        for row_tap in range(3):
            weight_copy(v, row_tap).wait()

        def step(k, carry):
            h = lax.rem(r + k, n_rows)
            for off in (-1, 0, 1):
                j = h + off
                first = n_rows
                for e in (-1, 0, 1):
                    user = j + e
                    turn = lax.rem(user - r + 2 * n_rows, n_rows)
                    valid = (user >= 0) & (user < n_rows)
                    first = jnp.minimum(first, jnp.where(valid, turn, n_rows))

                @pl.when((j >= 0) & (j < n_rows) & (j != r) & (first == k))
                def _():
                    act_arrival(v, 0, j).wait_recv()
                    act_arrival(v, 1, j).wait_recv()

            window = jnp.concatenate([abuf[v, h], abuf[v, h + 1], abuf[v, h + 2]], axis=1)
            kernel_all = wbuf[v].reshape(9 * lanes, 3 * chans)
            zbuf[...] = lax.dot_general(
                window, kernel_all, (((1,), (1,)), ((), ())), preferred_element_type=jnp.float32
            )

            def piece(f, tap, s):
                at = (3 * tap + s) * lanes
                return zbuf[f * width : (f + 1) * width, at : at + lanes]

            sides = []
            for tap in range(3):
                left = zbuf[cells : cells + 8, 3 * tap * lanes : (3 * tap + 1) * lanes]
                right = zbuf[cells : cells + 8, (3 * tap + 2) * lanes : (3 * tap + 3) * lanes]
                sides.append(jnp.where(c == 0, right, left))
            for g in range(frames + 2):
                taps = [tap for tap in range(3) if 0 <= g - 2 + tap < frames]
                left, mid, right = (
                    functools.reduce(jnp.add, [piece(g - 2 + tap, tap, s) for tap in taps]) for s in range(3)
                )
                side = functools.reduce(
                    jnp.add, [sides[tap][g - 2 + tap : g - 1 + tap, :] for tap in taps]
                )
                total = mid + jnp.where(column > 0, pltpu.roll(left, 1, 0), 0.0)
                total = total + jnp.where(column < width - 1, pltpu.roll(right, width - 1, 0), 0.0)
                total = total + jnp.where(column == edge_column, side, 0.0)
                if g < frames:
                    total = total + bias
                obuf[g * width : (g + 1) * width, :] = total
            main = obuf[0:block, :].astype(jnp.bfloat16)

            @pl.when(k == 0)
            def _():
                orecv[v, r] = main

            @pl.when(k > 0)
            def _():
                osend[v, h] = main
                out_copy(v, h, r).start()

            @pl.when(has_next)
            def _():
                psend[v, h] = obuf[cells : cells + 2 * width, :].astype(jnp.bfloat16)
                past_copy(v, h, r).start()

            return carry

        lax.fori_loop(0, n_rows, step, 0)
        for d in distances:
            j = lax.rem(r + d, n_rows)
            out_copy(v, j, j).wait_recv()

        @pl.when(has_prev)
        def _():
            for j in range(n_rows):
                past_copy(v, j, j).wait_recv()

        parts = []
        for j in range(n_rows):
            main = orecv[v, j].astype(jnp.float32)
            past = precv[v, j].astype(jnp.float32)
            part = jnp.concatenate([main[0 : 2 * width] + past, main[2 * width : cells]], axis=0)
            parts.append(part[:, 0:n_out])
        return jnp.concatenate(parts, axis=1)

    latents = x_ref[...].astype(jnp.float32).reshape(cells, chans)
    spread(0, activate(latents, gains[0][...]))
    first_out = convolve(0).astype(jnp.bfloat16).astype(jnp.float32)
    spread(1, activate(first_out, gains[1][...]))
    branch = convolve(1)
    latents = x_ref[...].astype(jnp.float32).reshape(cells, chans)
    out_ref[...] = (latents + branch).reshape(frames, 1, width, chans).astype(jnp.bfloat16)

    for v in range(2):
        edge_copy(v).wait_send()
        for d in distances:
            act_send(v, 0, d).wait_send()
            act_send(v, 1, d).wait_send()
            out_copy(v, lax.rem(r + d, n_rows), r).wait_send()

    @pl.when(has_next)
    def _():
        for v in range(2):
            for j in range(n_rows):
                past_copy(v, j, r).wait_send()


def solution(mesh):
    n_rows = mesh.shape["rows"]
    n_tm = mesh.shape["tm"]

    def shards(latents, gain_one, conv_one, bias_one, gain_two, conv_two, bias_two):
        frames, _, width, chans = latents.shape
        n_out = conv_one.shape[1]
        lanes = up(n_out, 128)
        block = up(frames * width + frames, 16)

        def taps(weight):
            weight = weight.reshape(3, 3, 3, n_out, chans)
            extra = up(n_out, 16) - n_out
            if extra:
                weight = jnp.pad(weight, ((0, 0), (0, 0), (0, 0), (0, extra), (0, 0)))
            return weight

        vmem = pl.BlockSpec(memory_space=pltpu.VMEM)
        hbm = pl.BlockSpec(memory_space=pl.ANY)
        dma = pltpu.SemaphoreType.DMA
        bf16 = jnp.bfloat16
        flops = 2 * 2 * n_rows * frames * width * 27 * chans * n_out
        return pl.pallas_call(
            functools.partial(kernel, n_rows, n_tm, n_out),
            out_shape=jax.ShapeDtypeStruct(latents.shape, bf16),
            in_specs=[vmem, vmem, hbm, vmem, vmem, hbm, vmem],
            out_specs=vmem,
            scratch_shapes=[
                pltpu.VMEM((2, n_rows + 2, block, chans), bf16),
                pltpu.VMEM((2, 3, 3, lanes, 3 * chans), bf16),
                pltpu.VMEM((block, 9 * lanes), jnp.float32),
                pltpu.VMEM((up((frames + 2) * width, 16), lanes), jnp.float32),
                pltpu.VMEM((2, n_rows, block, lanes), bf16),
                pltpu.VMEM((2, n_rows, 2 * width, lanes), bf16),
                pltpu.VMEM((2, n_rows, block, lanes), bf16),
                pltpu.VMEM((2, n_rows, 2 * width, lanes), bf16),
                pltpu.VMEM((2, 16, chans), bf16),
                pltpu.VMEM((2, 16, chans), bf16),
                dma((2, 3)),
                dma((2, 2, n_rows)),
                dma((2, 2, n_rows)),
                dma((2,)),
                dma((2,)),
                dma((2, n_rows)),
                dma((2, n_rows)),
                dma((2, n_rows)),
                dma((2, n_rows)),
            ],
            compiler_params=pltpu.CompilerParams(
                collective_id=0, has_side_effects=True, vmem_limit_bytes=48 * 1024 * 1024
            ),
            cost_estimate=pl.CostEstimate(flops=flops, bytes_accessed=8 * 1024 * 1024, transcendentals=0),
        )(
            latents,
            gain_one.reshape(1, chans),
            taps(conv_one),
            bias_one.reshape(1, chans),
            gain_two.reshape(1, chans),
            taps(conv_two),
            bias_two.reshape(1, chans),
        )

    return jax.shard_map(
        shards,
        mesh=mesh,
        in_specs=(
            P(("groups", "tm"), "rows", "cols", None),
            P(),
            P(None, "rows", None),
            P(),
            P(),
            P(None, "rows", None),
            P(),
        ),
        out_specs=P(("groups", "tm"), "rows", "cols", None),
        check_vma=False,
    )
```

time: 122 us -> 60.6 us (0.50)
  blocking collectives: 69.9 us -> 0 us
  Pallas kernels: 0 us -> 52.9 us
  starting transfers between devices: 17.7 us -> 0 us
  matrix products: 17.6 us -> 0 us
  waiting for transfers between devices: 3.79 us -> 0 us
  other arithmetic: 3.34 us -> 0 us
    pallas_call x0 -> x1, Pallas kernels: none -> 52.9 us  [shards(): pl.pallas_call(functools.partial(kernel, n_rows, n_tm, n_out), out_shape=...]
    all_gather x2 -> x0, blocking collectives: 44.4 us -> none  [convolve(): column = lax.all_gather(with_sides, 'rows', axis=1, tiled=True)]
    all_to_all x2 -> x0, blocking collectives: 25.5 us -> none  [convolve(): lax.all_to_all(result, 'rows', split_axis=1, concat_axis=3, tiled=True)]
    ppermute x6 -> x0, starting transfers between devices: 17.7 us -> none  [the longest x2 9.1 us: passed_along(): return lax.ppermute(block, axis, route)]
    dot_general x54 -> x0, matrix products: 17.6 us -> none  [tap_sum(): lax.dot_general(window, kernel, (((1,), (1,)), ((), ())), preferred_eleme...]
    slice x6 -> x0, local copies, waits for them, and re-layouts: 5.74 us -> none  [the longest x4 5.72 us: tap_sum(): padded[depth_tap:depth_tap + frames, row_tap:row_tap + height, col_tap:co...]
    unnamed x8 -> x7, local copies, waits for them, and re-layouts: 0.03 us -> 4.68 us
    ppermute x6 -> x0, waiting for transfers between devices: 3.79 us -> none  [the longest x2 3.69 us: passed_along(): return lax.ppermute(block, axis, route)]
  transfers between devices with their start and end apart: 6 -> 0, of which waited for: 2 -> 0; matrix products, arithmetic and copies ran while one was open for 1% -> 0% of each run, Pallas kernels for 0% -> 0%
where the time goes in v1:
time: 60.6 us; the launch traced here: 60.3 us
  Pallas kernels  52.9 us (87%)
  local copies, waits for them, and re-layouts  7.41 us (12%)
    pallas_call x1, Pallas kernels, shards(): pl.pallas_call(functools.partial(kernel, n_rows, n_tm, n_out), out_shape=...  52.9 us
    unnamed x7, local copies, waits for them, and re-layouts  4.68 us

profile of v1, /device:TPU:0, one launch (start us, length us, event | category | flops | bytes accessed | tf_op | source)
XLA Modules:
  0.0 60.3 jit_solution(2994349850859338447)
XLA Ops:
  0.0 0.7 %reshape.18.g1_ref = f32[1,384]{1,0:T(1,128)S(1)} reshape(f32[384]{0:T(512)} %param.8) | data formatting | bytes 3072 | tf_op jit(solution)/shard_map/reshape | solution.py:314
  0.7 0.7 %reshape.20.b1_ref = f32[1,384]{1,0:T(1,128)S(1)} reshape(f32[384]{0:T(512)} %param.10) | data formatting | bytes 3072 | tf_op jit(solution)/shard_map/reshape | solution.py:316
  1.4 0.7 %reshape.21.g2_ref = f32[1,384]{1,0:T(1,128)S(1)} reshape(f32[384]{0:T(512)} %param.11) | data formatting | bytes 3072 | tf_op jit(solution)/shard_map/reshape | solution.py:317
  2.0 0.7 %reshape.23.b2_ref = f32[1,384]{1,0:T(1,128)S(1)} reshape(f32[384]{0:T(512)} %param.13) | data formatting | bytes 3072 | tf_op jit(solution)/shard_map/reshape | solution.py:319
  2.7 0.0 copy-start
  2.7 1.6 %copy-done = bf16[27,96,384]{2,1,0:T(8,128)(2,1)S(1)} copy-done((bf16[27,96,384]{2,1,0:T(8,128)(2,1)S(1)}, bf16[27,96,384]{2,1,0:T(8,128)(2,1)}, u32[]{:S(2)}) %copy-start) | copy-done | bytes 1990680
  4.3 0.0 copy-start.1
  4.3 1.6 %copy-done.1 = bf16[27,96,384]{2,1,0:T(8,128)(2,1)S(1)} copy-done((bf16[27,96,384]{2,1,0:T(8,128)(2,1)S(1)}, bf16[27,96,384]{2,1,0:T(8,128)(2,1)}, u32[]{:S(2)}) %copy-start.1) | copy-done | bytes 1990680
  5.8 0.0 copy-start.2
  5.8 0.9 %copy-done.2 = bf16[5,1,40,384]{3,2,1,0:T(8,128)(2,1)S(1)} copy-done((bf16[5,1,40,384]{3,2,1,0:T(8,128)(2,1)S(1)}, bf16[5,1,40,384]{3,2,1,0:T(8,128)(2,1)}, u32[]{:S(2)}) %copy-start.2) | copy-done | bytes 153624
  6.8 52.9 %shard_map.73 = bf16[5,1,40,384]{3,2,1,0:T(8,128)(2,1)S(1)} custom-call(bf16[5,1,40,384]{3,2,1,0:T(8,128)(2,1)S(1)} %copy-done.2, f32[1,384]{1,0:T(1,128)S(1)} %reshape.18.g1_ref, bf16[3,3,3,96,384]{4,3,2,1,0:T(8,128)(2,1)S(1)} %bitcast.2, f32[1,384]{1,0:T(1,128)S(1)} %reshape.20.b1_ref, f32[1,384]{1,0:T(1,128)S(1)} %reshape.21.g2_ref, ...), custom_call_target="tpu_custom_call" | custom-call | flops 3185049600 | bytes 8388608 | tf_op jit(solution)/shard_map/pallas_call | solution.py:282
  59.6 0.7 %copy.9 = bf16[5,1,40,384]{3,2,1,0:T(8,128)(2,1)} copy(bf16[5,1,40,384]{3,2,1,0:T(8,128)(2,1)S(1)} %shard_map.73) | data formatting | bytes 307200
Async XLA Ops:
  2.7 1.6 %copy-start = (bf16[27,96,384]{2,1,0:T(8,128)(2,1)S(1)}, bf16[27,96,384]{2,1,0:T(8,128)(2,1)}, u32[]{:S(2)}) copy-start(bf16[27,96,384]{2,1,0:T(8,128)(2,1)} %param.9) | copy-start | bytes 5971972
  4.3 1.6 %copy-start.1 = (bf16[27,96,384]{2,1,0:T(8,128)(2,1)S(1)}, bf16[27,96,384]{2,1,0:T(8,128)(2,1)}, u32[]{:S(2)}) copy-start(bf16[27,96,384]{2,1,0:T(8,128)(2,1)} %param.12) | copy-start | bytes 5971972
  5.8 0.9 %copy-start.2 = (bf16[5,1,40,384]{3,2,1,0:T(8,128)(2,1)S(1)}, bf16[5,1,40,384]{3,2,1,0:T(8,128)(2,1)}, u32[]{:S(2)}) copy-start(bf16[5,1,40,384]{3,2,1,0:T(8,128)(2,1)} %x_ref.1) | copy-start | bytes 460804

commit v2 on v1

v2 whole, which is shorter than its diff:
```python
import functools

import jax
import jax.numpy as jnp
from jax import lax
from jax.experimental import pallas as pl
from jax.experimental.pallas import tpu as pltpu
from jax.sharding import PartitionSpec as P

MESH = pl.DeviceIdType.MESH
EPS = 1e-06


def up(value, multiple):
    return -(-value // multiple) * multiple


def activate(values, gain_values):
    mean_square = jnp.mean(values * values, axis=-1, keepdims=True)
    return jax.nn.silu(values * lax.rsqrt(mean_square + EPS) * gain_values)


def kernel(
    n_rows, n_tm, n_out, tail,
    x_hbm, g1_ref, w1_ref, b1_ref, g2_ref, w2_ref, b2_ref, out_ref, x_ref,
    abuf, bbuf, wbuf, zbuf, obuf, fbuf, osend, orecv, psend, precv,
    edge_out, edge_in, edges_out, edges_in,
    x_sem, w_sem, a_send, a_recv, e_send, e_recv, es_send, es_recv,
    f_send, f_recv, o_send, o_recv, p_send, p_recv,
):
    frames, _, width, chans = x_ref.shape
    cells = frames * width
    block = abuf.shape[1]
    head = block - 16
    lanes = wbuf.shape[3]
    packed = fbuf.shape[2]
    keep = cells - tail
    spare = lanes - n_out
    r = lax.axis_index("rows")
    t = lax.axis_index("tm")
    c = lax.axis_index("cols")
    weights = (w1_ref, w2_ref)
    biases = (b1_ref, b2_ref)
    acts = (abuf, bbuf)
    has_next = t + 1 < n_tm
    has_prev = t > 0
    distances = sorted(range(1, n_rows), key=lambda d: min(d, n_rows - d))

    def peer(d):
        return lax.rem(r + d, n_rows)

    def weight_copy(v, row_tap):
        return pltpu.make_async_copy(
            weights[v].at[:, row_tap],
            wbuf.at[v, :, :, pl.ds(0, weights[v].shape[3]), pl.ds(row_tap * chans, chans)],
            w_sem.at[v, row_tap],
        )

    def remote(src, dst, send, recv, where):
        return pltpu.make_async_remote_copy(
            src_ref=src, dst_ref=dst, send_sem=send, recv_sem=recv, device_id=where, device_id_type=MESH
        )

    fetch = pltpu.make_async_copy(x_hbm, x_ref, x_sem)
    fetch.start()
    for v in range(2):
        for row_tap in range(3):
            weight_copy(v, row_tap).start()

    barrier = pltpu.get_barrier_semaphore()

    def greet(where):
        pl.semaphore_signal(barrier, inc=1, device_id=where, device_id_type=MESH)

    for d in distances:
        greet({"rows": peer(d)})
    greet({"cols": 1 - c})

    @pl.when(has_next)
    def _():
        greet({"tm": t + 1})

    @pl.when(has_prev)
    def _():
        greet({"tm": t - 1})

    filled = weights[0].shape[3]
    for v in range(2):
        acts[v][0] = jnp.zeros((block, chans), jnp.bfloat16)
        acts[v][n_rows + 1] = jnp.zeros((block, chans), jnp.bfloat16)
        if filled < lanes:
            wbuf[v, :, :, filled:, :] = jnp.zeros((3, 3, lanes - filled, 3 * chans), jnp.bfloat16)

    @pl.when(t == 0)
    def _():
        precv[...] = jnp.zeros(precv.shape, precv.dtype)

    def edge_copy():
        return remote(edge_out, edge_in, e_send, e_recv, {"cols": 1 - c})

    def edges_copy(h):
        return remote(edges_out.at[h], edges_in.at[h], es_send.at[h], es_recv.at[h], {"cols": 1 - c})

    def span(piece):
        return pl.ds(0, head) if piece == 0 else pl.ds(head, 16)

    def act_copy(piece, source, d, where):
        part = abuf.at[source + 1, span(piece)]
        return remote(part, part, a_send.at[piece, d], a_recv.at[piece, source], {"rows": where})

    def first_copy(h, plane, d, where):
        part = fbuf.at[h, plane]
        return remote(part, part, f_send.at[h, d], f_recv.at[h, plane], {"rows": where})

    def out_copy(h, plane):
        return remote(osend.at[h], orecv.at[plane], o_send.at[h], o_recv.at[plane], {"rows": h})

    def past_copy(v, h):
        return remote(psend.at[v, h], precv.at[v, h], p_send.at[v, h], p_recv.at[v, h], {"tm": t + 1})

    def outer_column(act):
        cube = act.reshape(frames, width, chans)
        edge = jnp.where(c == 0, cube[:, width - 1, :], cube[:, 0, :])
        edge = jnp.concatenate([edge, jnp.zeros((16 - frames, chans), jnp.float32)], axis=0)
        return edge.astype(jnp.bfloat16)

    def pack(full):
        rows = full[0:keep]
        if tail:
            slices = [full[keep:cells, q * spare : (q + 1) * spare] for q in range(n_out // spare)]
            rest = keep - tail * len(slices)
            if rest:
                slices.append(jnp.zeros((rest, spare), jnp.float32))
            rows = jnp.concatenate([rows[:, 0:n_out], jnp.concatenate(slices, axis=0)], axis=1)
        if packed > keep:
            rows = jnp.concatenate([rows, jnp.zeros((packed - keep, lanes), jnp.float32)], axis=0)
        return rows.astype(jnp.bfloat16)

    def unpack(ref):
        rows = ref[...].astype(jnp.float32)
        main = rows[0:keep, 0:n_out]
        if tail:
            last = [rows[q * tail : (q + 1) * tail, n_out:lanes] for q in range(n_out // spare)]
            main = jnp.concatenate([main, jnp.concatenate(last, axis=1)], axis=0)
        return main

    def prepare(h):
        for d in distances:
            first_copy(h, peer(d), 0, r).wait_recv()
        first_out = jnp.concatenate([unpack(fbuf.at[h, j]) for j in range(n_rows)], axis=1)
        act = activate(first_out, g2_ref[...].reshape(1, chans))
        edges_out[h] = outer_column(act)
        edges_copy(h).start()
        rows = jnp.concatenate([act, jnp.zeros((block - cells, chans), jnp.float32)], axis=0)
        bbuf[h + 1] = rows.astype(jnp.bfloat16)

    def complete(h):
        edges_copy(h).wait_recv()
        rows = bbuf[h + 1, head:block].astype(jnp.float32)
        got = edges_in[h].astype(jnp.float32)
        rows = jnp.concatenate([rows[0 : cells - head], got[0 : block - cells]], axis=0)
        bbuf[h + 1, head:block] = rows.astype(jnp.bfloat16)

    def arrive(h):
        @pl.when(h != r)
        def _():
            for piece in range(2):
                act_copy(piece, h, 0, r).wait_recv()

    def convolve(v):
        bias_all = biases[v][...].reshape(1, chans)
        bias = jnp.zeros((1, n_out), jnp.float32)
        for j in range(n_rows):
            bias = bias + jnp.where(r == j, bias_all[:, j * n_out : (j + 1) * n_out], 0.0)
        if n_out < lanes:
            bias = jnp.concatenate([bias, jnp.zeros((1, lanes - n_out), jnp.float32)], axis=1)
        column = lax.broadcasted_iota(jnp.int32, (width, lanes), 0)
        edge_column = jnp.where(c == 0, width - 1, 0)

        def finish(h):
            @pl.when(has_prev)
            def _():
                past_copy(v, h).wait_recv()

            slot = lax.rem(h, 2)
            rows = obuf[slot, 0:cells]
            past = precv[v, h].astype(jnp.float32)
            rows = jnp.concatenate([rows[0 : 2 * width] + past, rows[2 * width : cells]], axis=0)
            rows = pack(rows + bias)
            if v == 0:
                fbuf[h, r] = rows
                for d in distances:
                    first_copy(h, r, d, peer(d)).start()
            else:
                @pl.when(h == r)
                def _():
                    orecv[r] = rows

                @pl.when(h != r)
                def _():
                    osend[h] = rows
                    out_copy(h, r).start()

        get = arrive if v == 0 else prepare
        get(0)
        for row_tap in range(3):
            weight_copy(v, row_tap).wait()
        if v == 1:
            complete(0)

        def step(h, carry):
            more = h + 1 < n_rows

            @pl.when(more)
            def _():
                get(h + 1)

            @pl.when(h > 0)
            def _():
                finish(h - 1)

            if v == 1:
                @pl.when(more)
                def _():
                    complete(h + 1)

            source = acts[v]
            window = jnp.concatenate([source[h], source[h + 1], source[h + 2]], axis=1)
            kernel_all = wbuf[v].reshape(9 * lanes, 3 * chans)
            zbuf[...] = lax.dot_general(
                window, kernel_all, (((1,), (1,)), ((), ())), preferred_element_type=jnp.float32
            )
            slot = lax.rem(h, 2)

            def piece(f, tap, s):
                at = (3 * tap + s) * lanes
                return zbuf[f * width : (f + 1) * width, at : at + lanes]

            sides = []
            for tap in range(3):
                left = zbuf[cells : cells + 8, 3 * tap * lanes : (3 * tap + 1) * lanes]
                right = zbuf[cells : cells + 8, (3 * tap + 2) * lanes : (3 * tap + 3) * lanes]
                sides.append(jnp.where(c == 0, right, left))
            for g in (*range(frames, frames + 2), *range(frames)):
                taps = [tap for tap in range(3) if 0 <= g - 2 + tap < frames]
                left, mid, right = (
                    functools.reduce(jnp.add, [piece(g - 2 + tap, tap, s) for tap in taps]) for s in range(3)
                )
                side = functools.reduce(
                    jnp.add, [sides[tap][g - 2 + tap : g - 1 + tap, :] for tap in taps]
                )
                total = mid + jnp.where(column > 0, pltpu.roll(left, 1, 0), 0.0)
                total = total + jnp.where(column < width - 1, pltpu.roll(right, width - 1, 0), 0.0)
                total = total + jnp.where(column == edge_column, side, 0.0)
                obuf[slot, g * width : (g + 1) * width, :] = total
                if g == frames + 1:
                    @pl.when(has_next)
                    def _():
                        psend[v, h] = obuf[slot, cells : cells + 2 * width, :].astype(jnp.bfloat16)
                        past_copy(v, h).start()

            return carry

        lax.fori_loop(0, n_rows, step, 0)
        finish(n_rows - 1)

    fetch.wait()
    act = activate(
        x_ref[...].astype(jnp.float32).reshape(cells, chans), g1_ref[...].reshape(1, chans)
    )
    edge_out[...] = outer_column(act)
    pl.semaphore_wait(
        barrier, n_rows + jnp.where(has_next, 1, 0) + jnp.where(has_prev, 1, 0)
    )
    edge_copy().start()
    abuf[r + 1, 0:head] = act[0:head].astype(jnp.bfloat16)
    for d in distances:
        act_copy(0, r, d, peer(d)).start()
    edge_copy().wait_recv()
    got = edge_in[...].astype(jnp.float32)
    last = jnp.concatenate([act[head:cells], got[0 : block - cells]], axis=0)
    abuf[r + 1, head:block] = last.astype(jnp.bfloat16)
    for d in distances:
        act_copy(1, r, d, peer(d)).start()

    convolve(0)
    convolve(1)

    for d in distances:
        j = peer(d)
        out_copy(j, j).wait_recv()
    branch = jnp.concatenate([unpack(orecv.at[j]) for j in range(n_rows)], axis=1)
    latents = x_ref[...].astype(jnp.float32).reshape(cells, chans)
    out_ref[...] = (latents + branch).reshape(frames, 1, width, chans).astype(jnp.bfloat16)

    edge_copy().wait_send()
    for d in distances:
        for piece in range(2):
            act_copy(piece, r, d, peer(d)).wait_send()
        out_copy(peer(d), r).wait_send()

    def drain(h, carry):
        edges_copy(h).wait_send()
        for d in distances:
            first_copy(h, r, d, peer(d)).wait_send()

        @pl.when(has_next)
        def _():
            for v in range(2):
                past_copy(v, h).wait_send()

        return carry

    lax.fori_loop(0, n_rows, drain, 0)


def solution(mesh):
    n_rows = mesh.shape["rows"]
    n_tm = mesh.shape["tm"]

    def shards(latents, gain_one, conv_one, bias_one, gain_two, conv_two, bias_two):
        frames, _, width, chans = latents.shape
        n_out = conv_one.shape[1]
        lanes = up(n_out, 128)
        cells = frames * width
        block = up(cells + frames, 16)
        spare = lanes - n_out
        tail = 0
        if spare and n_out % spare == 0:
            tail = cells // (n_out // spare + 1) // 8 * 8
        packed = up(cells - tail, 16)

        def taps(weight):
            weight = weight.reshape(3, 3, 3, n_out, chans)
            extra = up(n_out, 16) - n_out
            if extra:
                weight = jnp.pad(weight, ((0, 0), (0, 0), (0, 0), (0, extra), (0, 0)))
            return weight

        vmem = pl.BlockSpec(memory_space=pltpu.VMEM)
        hbm = pl.BlockSpec(memory_space=pl.ANY)
        dma = pltpu.SemaphoreType.DMA
        bf16 = jnp.bfloat16
        flops = 2 * 2 * n_rows * frames * width * 27 * chans * n_out
        return pl.pallas_call(
            functools.partial(kernel, n_rows, n_tm, n_out, tail),
            out_shape=jax.ShapeDtypeStruct(latents.shape, bf16),
            in_specs=[hbm, vmem, hbm, vmem, vmem, hbm, vmem],
            out_specs=vmem,
            scratch_shapes=[
                pltpu.VMEM(latents.shape, bf16),
                pltpu.VMEM((n_rows + 2, block, chans), bf16),
                pltpu.VMEM((n_rows + 2, block, chans), bf16),
                pltpu.VMEM((2, 3, 3, lanes, 3 * chans), bf16),
                pltpu.VMEM((block, 9 * lanes), jnp.float32),
                pltpu.VMEM((2, up((frames + 2) * width, 16), lanes), jnp.float32),
                pltpu.VMEM((n_rows, n_rows, packed, lanes), bf16),
                pltpu.VMEM((n_rows, packed, lanes), bf16),
                pltpu.VMEM((n_rows, packed, lanes), bf16),
                pltpu.VMEM((2, n_rows, 2 * width, lanes), bf16),
                pltpu.VMEM((2, n_rows, 2 * width, lanes), bf16),
                pltpu.VMEM((16, chans), bf16),
                pltpu.VMEM((16, chans), bf16),
                pltpu.VMEM((n_rows, 16, chans), bf16),
                pltpu.VMEM((n_rows, 16, chans), bf16),
                dma,
                dma((2, 3)),
                dma((2, n_rows)),
                dma((2, n_rows)),
                dma,
                dma,
                dma((n_rows,)),
                dma((n_rows,)),
                dma((n_rows, n_rows)),
                dma((n_rows, n_rows)),
                dma((n_rows,)),
                dma((n_rows,)),
                dma((2, n_rows)),
                dma((2, n_rows)),
            ],
            compiler_params=pltpu.CompilerParams(
                collective_id=0, has_side_effects=True, vmem_limit_bytes=60 * 1024 * 1024
            ),
            cost_estimate=pl.CostEstimate(flops=flops, bytes_accessed=8 * 1024 * 1024, transcendentals=0),
        )(
            latents,
            gain_one,
            taps(conv_one),
            bias_one,
            gain_two,
            taps(conv_two),
            bias_two,
        )

    return jax.shard_map(
        shards,
        mesh=mesh,
        in_specs=(
            P(("groups", "tm"), "rows", "cols", None),
            P(),
            P(None, "rows", None),
            P(),
            P(),
            P(None, "rows", None),
            P(),
        ),
        out_specs=P(("groups", "tm"), "rows", "cols", None),
        check_vma=False,
    )
```

time: 60.6 us -> 48.8 us (0.81)
  the two profiles are of different devices: /device:TPU:0 before, /device:TPU:26 now
where the time goes in v2:
time: 48.8 us; the launch traced here: 48.6 us
  Pallas kernels  47 us (96%)
  local copies, waits for them, and re-layouts  1.59 us (3%)
    pallas_call x1, Pallas kernels, shards(): pl.pallas_call(functools.partial(kernel, n_rows, n_tm, n_out, tail), out_...  47 us
    unnamed x1, local copies, waits for them, and re-layouts  1.59 us

profile of v2, /device:TPU:26, one launch (start us, length us, event | category | flops | bytes accessed | tf_op | source)
XLA Modules:
  0.0 48.6 jit_solution(2878749277123861515)
XLA Ops:
  0.0 47.0 %shard_map.73 = bf16[5,1,40,384]{3,2,1,0:T(8,128)(2,1)} custom-call(bf16[5,1,40,384]{3,2,1,0:T(8,128)(2,1)} %x_hbm.1, f32[384]{0:T(512)} %g1_ref.1, bf16[3,3,3,96,384]{4,3,2,1,0:T(8,128)(2,1)} %bitcast.2, f32[384]{0:T(512)} %b1_ref.1, f32[384]{0:T(512)} %g2_ref.1, bf16[3,3,3,96,384]{4,3,2,1,0:T(8,128)(2,1)} %bitcast.3, f32[384]{0:T(512)} %b2_ref.1), custom_call_target="tpu_custom_call" | custom-call | flops 3185049600 | bytes 8388608 | tf_op jit(solution)/shard_map/pallas_call | solution.py:345
  47.0 1.6 %copy.9 = bf16[5,1,40,384]{3,2,1,0:T(8,128)(2,1)} copy(bf16[5,1,40,384]{3,2,1,0:T(8,128)(2,1)} %shard_map.73) | data formatting | bytes 307200

commit v3 on v2

--- a/solution.py
+++ b/solution.py
@@ -26,12 +26,15 @@
     abuf, bbuf, wbuf, zbuf, obuf, fbuf, osend, orecv, psend, precv,
     edge_out, edge_in, edges_out, edges_in,
     x_sem, w_sem, a_send, a_recv, e_send, e_recv, es_send, es_recv,
-    f_send, f_recv, o_send, o_recv, p_send, p_recv,
+    ra_send, rf_send, f_send, f_recv, o_send, o_recv, p_send, p_recv,
 ):
     frames, _, width, chans = x_ref.shape
     cells = frames * width
     block = abuf.shape[1]
     head = block - 16
+    third = up(-(-head // 3), 16)
+    pieces = [(at, min(third, head - at)) for at in range(0, head, third)] + [(head, 16)]
+    far = len(pieces) - 1
     lanes = wbuf.shape[3]
     packed = fbuf.shape[2]
     keep = cells - tail
@@ -101,12 +104,41 @@
     def edges_copy(h):
         return remote(edges_out.at[h], edges_in.at[h], es_send.at[h], es_recv.at[h], {"cols": 1 - c})
 
+    offsets = (2, -2, 1, -1)
+
+    def inside(j):
+        return (j >= 0) & (j < n_rows)
+
+    def relayed(s):
+        return ((s <= r - 2) & (r + 1 < n_rows)) | ((s >= r + 2) & (r >= 1))
+
+    def near(action):
+        for o in offsets:
+            @pl.when(inside(r + o))
+            def _(o=o):
+                action(o + 2, r + o)
+
+    def relays(action):
+        for distance in range(2, n_rows):
+            for sign in (1, -1):
+                @pl.when(inside(r - sign * distance) & inside(r + sign))
+                def _(distance=distance, sign=sign):
+                    action(r - sign * distance, r + sign)
+
     def span(piece):
-        return pl.ds(0, head) if piece == 0 else pl.ds(head, 16)
+        return pl.ds(*pieces[piece])
 
     def act_copy(piece, source, d, where):
         part = abuf.at[source + 1, span(piece)]
         return remote(part, part, a_send.at[piece, d], a_recv.at[piece, source], {"rows": where})
+
+    def act_relay(piece, source, where):
+        part = abuf.at[source + 1, span(piece)]
+        return remote(part, part, ra_send.at[piece, source], a_recv.at[piece, source], {"rows": where})
+
+    def first_relay(h, plane, where):
+        part = fbuf.at[h, plane]
+        return remote(part, part, rf_send.at[h, plane], f_recv.at[h, plane], {"rows": where})
 
     def first_copy(h, plane, d, where):
         part = fbuf.at[h, plane]
@@ -145,8 +177,10 @@
         return main
 
     def prepare(h):
-        for d in distances:
-            first_copy(h, peer(d), 0, r).wait_recv()
+        for j in range(n_rows):
+            @pl.when((r != j) & jnp.logical_not(relayed(j)))
+            def _(j=j):
+                first_copy(h, j, 0, r).wait_recv()
         first_out = jnp.concatenate([unpack(fbuf.at[h, j]) for j in range(n_rows)], axis=1)
         act = activate(first_out, g2_ref[...].reshape(1, chans))
         edges_out[h] = outer_column(act)
@@ -162,10 +196,25 @@
         bbuf[h + 1, head:block] = rows.astype(jnp.bfloat16)
 
     def arrive(h):
-        @pl.when(h != r)
+        @pl.when((h != r) & jnp.logical_not(relayed(h)))
         def _():
-            for piece in range(2):
+            for piece in range(len(pieces)):
                 act_copy(piece, h, 0, r).wait_recv()
+
+    def relay_acts():
+        for piece in range(len(pieces)):
+            def hand_on(source, where):
+                act_copy(piece, source, 0, r).wait_recv()
+                act_relay(piece, source, where).start()
+
+            relays(hand_on)
+
+    def relay_first(h):
+        def hand_on(source, where):
+            first_copy(h, source, 0, r).wait_recv()
+            first_relay(h, source, where).start()
+
+        relays(hand_on)
 
     def convolve(v):
         bias_all = biases[v][...].reshape(1, chans)
@@ -189,8 +238,7 @@
             rows = pack(rows + bias)
             if v == 0:
                 fbuf[h, r] = rows
-                for d in distances:
-                    first_copy(h, r, d, peer(d)).start()
+                near(lambda d, where: first_copy(h, r, d, where).start())
             else:
                 @pl.when(h == r)
                 def _():
@@ -210,6 +258,10 @@
 
         def step(h, carry):
             more = h + 1 < n_rows
+            if v == 1:
+                @pl.when(h < min(2, n_rows))
+                def _():
+                    relay_first(n_rows - min(2, n_rows) + h)
 
             @pl.when(more)
             def _():
@@ -218,6 +270,11 @@
             @pl.when(h > 0)
             def _():
                 finish(h - 1)
+
+            if v == 0:
+                @pl.when(h > 1)
+                def _():
+                    relay_first(h - 2)
 
             if v == 1:
                 @pl.when(more)
@@ -274,14 +331,14 @@
     )
     edge_copy().start()
     abuf[r + 1, 0:head] = act[0:head].astype(jnp.bfloat16)
-    for d in distances:
-        act_copy(0, r, d, peer(d)).start()
+    for piece in range(far):
+        near(lambda d, where: act_copy(piece, r, d, where).start())
     edge_copy().wait_recv()
     got = edge_in[...].astype(jnp.float32)
     last = jnp.concatenate([act[head:cells], got[0 : block - cells]], axis=0)
     abuf[r + 1, head:block] = last.astype(jnp.bfloat16)
-    for d in distances:
-        act_copy(1, r, d, peer(d)).start()
+    near(lambda d, where: act_copy(far, r, d, where).start())
+    relay_acts()
 
     convolve(0)
     convolve(1)
@@ -294,15 +351,16 @@
     out_ref[...] = (latents + branch).reshape(frames, 1, width, chans).astype(jnp.bfloat16)
 
     edge_copy().wait_send()
+    for piece in range(len(pieces)):
+        near(lambda d, where: act_copy(piece, r, d, where).wait_send())
+        relays(lambda source, where: act_relay(piece, source, where).wait_send())
     for d in distances:
-        for piece in range(2):
-            act_copy(piece, r, d, peer(d)).wait_send()
         out_copy(peer(d), r).wait_send()
 
     def drain(h, carry):
         edges_copy(h).wait_send()
-        for d in distances:
-            first_copy(h, r, d, peer(d)).wait_send()
+        near(lambda d, where: first_copy(h, r, d, where).wait_send())
+        relays(lambda source, where: first_relay(h, source, where).wait_send())
 
         @pl.when(has_next)
         def _():
@@ -365,13 +423,15 @@
                 pltpu.VMEM((n_rows, 16, chans), bf16),
                 dma,
                 dma((2, 3)),
-                dma((2, n_rows)),
-                dma((2, n_rows)),
+                dma((4, 5)),
+                dma((4, n_rows)),
                 dma,
                 dma,
                 dma((n_rows,)),
                 dma((n_rows,)),
+                dma((4, n_rows)),
                 dma((n_rows, n_rows)),
+                dma((n_rows, 5)),
                 dma((n_rows, n_rows)),
                 dma((n_rows,)),
                 dma((n_rows,)),

time: 48.8 us -> 44.1 us (0.904)
  Pallas kernels: 47 us -> 42.3 us
    pallas_call x1, Pallas kernels: 47 us -> 42.3 us  [shards(): pl.pallas_call(functools.partial(kernel, n_rows, n_tm, n_out, tail), out_...]
where the time goes in v3:
time: 44.1 us; the launch traced here: 43.9 us
  Pallas kernels  42.3 us (96%)
  local copies, waits for them, and re-layouts  1.59 us (4%)
    pallas_call x1, Pallas kernels, shards(): pl.pallas_call(functools.partial(kernel, n_rows, n_tm, n_out, tail), out_...  42.3 us
    unnamed x1, local copies, waits for them, and re-layouts  1.59 us

profile of v3, /device:TPU:26, one launch (start us, length us, event | category | flops | bytes accessed | tf_op | source)
XLA Modules:
  0.0 43.9 jit_solution(17329817985575550963)
XLA Ops:
  0.0 42.3 %shard_map.73 = bf16[5,1,40,384]{3,2,1,0:T(8,128)(2,1)} custom-call(bf16[5,1,40,384]{3,2,1,0:T(8,128)(2,1)} %x_hbm.1, f32[384]{0:T(512)} %g1_ref.1, bf16[3,3,3,96,384]{4,3,2,1,0:T(8,128)(2,1)} %bitcast.2, f32[384]{0:T(512)} %b1_ref.1, f32[384]{0:T(512)} %g2_ref.1, bf16[3,3,3,96,384]{4,3,2,1,0:T(8,128)(2,1)} %bitcast.3, f32[384]{0:T(512)} %b2_ref.1), custom_call_target="tpu_custom_call" | custom-call | flops 3185049600 | bytes 8388608 | tf_op jit(solution)/shard_map/pallas_call | solution.py:403
  42.3 1.6 %copy.9 = bf16[5,1,40,384]{3,2,1,0:T(8,128)(2,1)} copy(bf16[5,1,40,384]{3,2,1,0:T(8,128)(2,1)} %shard_map.73) | data formatting | bytes 307200

commit v4 on v3

--- a/solution.py
+++ b/solution.py
@@ -271,22 +271,33 @@
             def _():
                 finish(h - 1)
 
-            if v == 0:
-                @pl.when(h > 1)
-                def _():
-                    relay_first(h - 2)
-
             if v == 1:
                 @pl.when(more)
                 def _():
                     complete(h + 1)
 
             source = acts[v]
-            window = jnp.concatenate([source[h], source[h + 1], source[h + 2]], axis=1)
-            kernel_all = wbuf[v].reshape(9 * lanes, 3 * chans)
-            zbuf[...] = lax.dot_general(
-                window, kernel_all, (((1,), (1,)), ((), ())), preferred_element_type=jnp.float32
-            )
+
+            def multiply(first, count):
+                window = jnp.concatenate([source[h + first + q] for q in range(count)], axis=1)
+                taps = wbuf[v, :, :, :, first * chans : (first + count) * chans]
+                zbuf[...] = lax.dot_general(
+                    window, taps.reshape(9 * lanes, count * chans), (((1,), (1,)), ((), ())),
+                    preferred_element_type=jnp.float32,
+                )
+
+            @pl.when(h == 0)
+            def _():
+                multiply(1, 2)
+
+            @pl.when((h > 0) & more)
+            def _():
+                multiply(0, 3)
+
+            @pl.when((h > 0) & jnp.logical_not(more))
+            def _():
+                multiply(0, 2)
+
             slot = lax.rem(h, 2)
 
             def piece(f, tap, s):
@@ -315,6 +326,11 @@
                     def _():
                         psend[v, h] = obuf[slot, cells : cells + 2 * width, :].astype(jnp.bfloat16)
                         past_copy(v, h).start()
+
+            if v == 0:
+                @pl.when(h > 1)
+                def _():
+                    relay_first(h - 2)
 
             return carry
 

time: 44.1 us -> 43.5 us (0.986)
  Pallas kernels: 42.3 us -> 41.8 us
    pallas_call x1, Pallas kernels: 42.3 us -> 41.8 us  [shards(): pl.pallas_call(functools.partial(kernel, n_rows, n_tm, n_out, tail), out_...]
where the time goes in v4:
time: 43.5 us; the launch traced here: 43.4 us
  Pallas kernels  41.8 us (96%)
  local copies, waits for them, and re-layouts  1.59 us (4%)
    pallas_call x1, Pallas kernels, shards(): pl.pallas_call(functools.partial(kernel, n_rows, n_tm, n_out, tail), out_...  41.8 us
    unnamed x1, local copies, waits for them, and re-layouts  1.59 us

profile of v4, /device:TPU:26, one launch (start us, length us, event | category | flops | bytes accessed | tf_op | source)
XLA Modules:
  0.0 43.4 jit_solution(696783513383370952)
XLA Ops:
  0.0 41.8 %shard_map.73 = bf16[5,1,40,384]{3,2,1,0:T(8,128)(2,1)} custom-call(bf16[5,1,40,384]{3,2,1,0:T(8,128)(2,1)} %x_hbm.1, f32[384]{0:T(512)} %g1_ref.1, bf16[3,3,3,96,384]{4,3,2,1,0:T(8,128)(2,1)} %bitcast.2, f32[384]{0:T(512)} %b1_ref.1, f32[384]{0:T(512)} %g2_ref.1, bf16[3,3,3,96,384]{4,3,2,1,0:T(8,128)(2,1)} %bitcast.3, f32[384]{0:T(512)} %b2_ref.1), custom_call_target="tpu_custom_call" | custom-call | flops 3185049600 | bytes 8388608 | tf_op jit(solution)/shard_map/pallas_call | solution.py:419
  41.8 1.6 %copy.9 = bf16[5,1,40,384]{3,2,1,0:T(8,128)(2,1)} copy(bf16[5,1,40,384]{3,2,1,0:T(8,128)(2,1)} %shard_map.73) | data formatting | bytes 307200
